TPU v7x, 256 devices: a whole 4x4x8 slice. The times are simulated.
256 devices in a mesh: query: 16 (over x_hi, z), feat: 16 (over x_lo, y, core).
Axes of the slice: x: 4 (x_hi: 2, x_lo: 2; x = x_hi * 2 + x_lo), y: 4, z: 8, core: 2. Of those that a mesh axis runs over, the one named last changes fastest.
Arguments:
- query_grads: bfloat16 [8192, 65536], P('query', 'feat'), may hold values from -6 to 6
- train_grads: bfloat16 [2048, 65536], P('query', 'feat'), may hold values from -0.03125 to 0.03125
- eigenvalues: float32 [65536], P('feat'), may hold values from 0.05 to 5
- offsets: int32 [33], replicated, may hold values from 0 to 65536, as said below
Outputs:
- scores: float32 [2048, 8192], P('feat', 'query')
Inputs may be any that keep to these rules, and one draw needn't show every extreme that they name: offsets[0] = 0, offsets[32] = 65536, strictly increasing; each block holds between 1536 and 2560 features.
All inputs are finite; a program needn't handle non-finite values.
Results may differ from a plain program's by a relative error of at most 0.0029.
Values may be sent and summed in bfloat16 or wider, within the bound.
A program may use at most 64 MiB of HBM per device.

v0:
```python
import jax
import jax.numpy as jnp
from jax import lax
from jax.sharding import PartitionSpec as P

F = 65536


def layer_table(feature_ids, offsets):
    return (
        (feature_ids[:, None] >= offsets[None, :-1]) & (feature_ids[:, None] < offsets[None, 1:])
    ).astype(jnp.float32)


def per_device(query_grads, train_grads, eigenvalues, offsets):
    local_width = eigenvalues.shape[0]
    first = lax.axis_index("feat") * local_width
    local_ids = first + jnp.arange(local_width, dtype=jnp.int32)
    onehot = layer_table(local_ids, offsets)
    every_eigen = lax.all_gather(eigenvalues, "feat", axis=0, tiled=True)
    every_ids = jnp.arange(every_eigen.shape[0], dtype=jnp.int32)
    layer_sum = jnp.dot(
        every_eigen, layer_table(every_ids, offsets), precision=lax.Precision.HIGHEST
    )
    total = jnp.sum(layer_sum)
    counts = (offsets[1:] - offsets[:-1]).astype(jnp.float32)
    damping = 0.05 * (layer_sum / counts + total / F)
    damp_feat = jnp.dot(onehot, damping, precision=lax.Precision.HIGHEST)
    weight = 1.0 / (eigenvalues + damp_feat)
    preconditioned = (train_grads.astype(jnp.float32) * weight[None, :]).astype(jnp.bfloat16)
    partial_scores = lax.dot_general(
        lax.all_gather(preconditioned, "query", axis=0, tiled=True),
        query_grads,
        (((1,), (1,)), ((), ())),
        preferred_element_type=jnp.float32,
    )
    return lax.psum_scatter(partial_scores, "feat", scatter_dimension=0, tiled=True)


def solution(mesh):
    return jax.shard_map(
        per_device,
        mesh=mesh,
        in_specs=(P("query", "feat"), P("query", "feat"), P("feat"), P()),
        out_specs=P("feat", "query"),
        check_vma=False,
    )
```

profile of v0, /device:TPU:17, one launch (start us, length us, event | category | flops | bytes accessed | tf_op | source)
XLA Modules:
  0.0 343.8 jit_solution(15784115449226786408)
XLA Ops:
  6.5 0.0 copy-start.1
  6.5 0.0 copy-start
  6.5 0.0 all-gather.2.cloned.1.call-start
  6.5 0.8 fusion.17
  7.4 18.1 %all_gather.6 = f32[65536]{0:T(1024)S(1)} all-gather(f32[4096]{0:T(1024)} %param.6), channel_id=1, replica_groups=mesh['query'=16,'feat'=16] {'feat'}, dimensions={0}, use_global_device_ids=true | all-gather | bytes 278528 | tf_op jit(solution)/shard_map/all_gather | solution.py:20
  25.4 5.4 %fusion.18 = (f32[]{:T(128)}, f32[32]{0:T(128)S(1)}) fusion(f32[65536,1]{0,1:T(1,128)S(1)} %bitcast.10, s32[32]{0:T(128)S(1)} %get-tuple-element.6, s32[32]{0:T(128)S(1)} %get-tuple-element.5), kind=kOutput, calls=%fused_computation.23 | convolution fusion | flops 31457312 | bytes 262532 | tf_op jit(solution)/shard_map/dot_general | solution.py:22
  31.5 0.4 fusion.8
  31.9 0.0 copy-done.1
  31.9 0.0 copy-done
  31.9 1.2 multiply_convert_fusion
  33.1 0.0 all-gather.2.cloned.1.call-update
  33.1 0.0 reduce-scatter.2.cloned.1.call-start
  33.1 227.3 %all-gather.2.cloned.1.call-done = bf16[2048,4096]{1,0:T(8,128)(2,1)} async-done(((bf16[128,4096]{1,0:T(8,128)(2,1)}), bf16[2048,4096]{1,0:T(8,128)(2,1)}) %all-gather.2.cloned.1.call-update) | async-done | bytes 16777232 | tf_op jit(solution)/shard_map/all_gather | solution.py:32
  260.5 14.9 %fusion.19 = f32[2048,512]{1,0:T(8,128)} fusion(bf16[2048,4096]{1,0:T(8,128)(2,1)} %all-gather.2.cloned.1.call-done, bf16[512,4096]{1,0:T(8,128)(2,1)} %param.4), kind=kOutput, calls=%fused_computation.24 | convolution fusion | flops 8589934592 | bytes 25165824 | tf_op jit(solution)/shard_map/dot_general | solution.py:31
  275.4 0.0 reduce-scatter.2.cloned.1.call-update
  275.4 61.5 %reduce-scatter.2.cloned.1.call-done = f32[128,512]{1,0:T(8,128)} async-done(((f32[2048,512]{1,0:T(8,128)}), f32[128,512]{1,0:T(8,128)}) %reduce-scatter.2.cloned.1.call-update) | async-done | bytes 262160 | tf_op jit(solution)/shard_map/reduce_scatter | solution.py:37
  (2 shorter events, 0.0 us)
Async XLA Ops:
  6.5 25.3 %copy-start.1 = (f32[4096]{0:T(1024)S(1)}, f32[4096]{0:T(1024)}, u32[]{:S(2)}) copy-start(f32[4096]{0:T(1024)} %param.6) | copy-start | bytes 49156
  6.5 25.3 %copy-start = (bf16[128,4096]{1,0:T(8,128)(2,1)S(1)}, bf16[128,4096]{1,0:T(8,128)(2,1)}, u32[]{:S(2)}) copy-start(bf16[128,4096]{1,0:T(8,128)(2,1)} %param.5) | copy-start | bytes 3145732
  6.5 253.9 %all-gather.2.cloned.1.call-start = ((), (), s32[]{:S(2)}) async-start(), calls=%async_computation.1 | async-start | bytes 17825792 | tf_op jit(solution)/shard_map/all_gather | solution.py:32
  33.1 303.9 %reduce-scatter.2.cloned.1.call-start = ((), (), s32[]{:S(2)}) async-start(), calls=%async_computation.2 | async-start | bytes 4456448 | tf_op jit(solution)/shard_map/reduce_scatter | solution.py:37
Sparse Core Ops, SparseCore 0:
  33.2 227.2 all-gather.1
  275.5 61.3 reduce-scatter.1
where the time goes:
time: 349 us; the launch traced here: 344 us
  waiting for transfers between devices  289 us (83%)
  matrix products  20.7 us (6%)
  blocking collectives  18.1 us (5%)
  between operations  14.1 us (4%)
    all_gather x1, waiting for transfers between devices, per_device(): lax.all_gather(preconditioned, 'query', axis=0, tiled=True)  227 us
    reduce_scatter x1, waiting for transfers between devices, per_device(): lax.psum_scatter(partial_scores, 'feat', scatter_dimension=0, tiled=True)  61.5 us
    all_gather x1, blocking collectives, per_device(): every_eigen = lax.all_gather(eigenvalues, 'feat', axis=0, tiled=True)  18.1 us
    dot_general x1, matrix products, per_device(): lax.dot_general(lax.all_gather(preconditioned, 'query', axis=0, tiled=Tru...  14.9 us
  transfers between devices with their start and end apart: 2, of which 2 were waited for; matrix products, arithmetic and copies ran while one was open for 0% of the time, Pallas kernels for 0%

commit v1 on v0

v1 whole, which is shorter than its diff:
```python
import functools

import jax
import jax.numpy as jnp
from jax import lax
from jax.experimental import pallas as pl
from jax.experimental.pallas import tpu as pltpu
from jax.sharding import PartitionSpec as P

MESH = pl.DeviceIdType.MESH
F = 65536
LAYERS = 32
ZS = 8
FEATS = 16
CHIPS = 16
WIDTH = 4096
ROWS = 128
QROWS = 512
CHUNK = 32
PAIR = 2 * CHUNK
PAIRS = 16
STEPS = PAIRS - 2
QPARTS = 8
QCHUNK = QROWS // QPARTS
GROUP = 4
BOTH = 12


def rows(start, size):
    return pl.ds(pl.multiple_of(start, size), size)


def kernel(
    offs, q_hbm, t_hbm, e_hbm, out,
    g, w, qb, pb, rb, wt, eb, ls,
    own_recv, t_send, r_send, r_recv, l_send, l_recv,
    home_recv, home_send, away_recv, away_send, fwd_send,
    e_copy, e_send, e_recv, ls_send, ls_recv, o_send, o_recv,
):
    qi, fi = lax.axis_index("query"), lax.axis_index("feat")
    xh, z = qi // ZS, qi % ZS
    xl, y, c = fi // 8, (fi // 2) % 4, fi % 2
    slot = (xh * 2 + xl) * 4 + y
    native = c == xh
    foreign = c != xh
    right = (xh * ZS + (z + 1) % ZS, fi)
    left = (xh * ZS + (z + ZS - 1) % ZS, fi)
    sibling = (qi, fi + 1 - 2 * c)
    partner = ((1 - xh) * ZS + z, fi + 1 - 2 * c)

    def remote(src, dst, send, recv, device):
        return pltpu.make_async_remote_copy(
            src_ref=src, dst_ref=dst, send_sem=send, recv_sem=recv, device_id=device, device_id_type=MESH
        )

    def arrived(ref, sem):
        pltpu.make_async_copy(ref, ref, sem).wait()

    def loop(low, high, body):
        def step(i, carry):
            body(i)
            return carry

        lax.fori_loop(low, high, step, 0)

    def own_rows(i):
        return rows(i * CHUNK, CHUNK)

    def q_rows(i):
        return rows(i * QCHUNK, QCHUNK)

    def local_t(i):
        return pltpu.make_async_copy(t_hbm.at[own_rows(i)], g.at[own_rows(i)], own_recv.at[i])

    def local_q(i):
        return pltpu.make_async_copy(q_hbm.at[q_rows(i)], qb.at[0, q_rows(i)], home_recv.at[i])

    local_e = pltpu.make_async_copy(e_hbm, eb.at[c], e_copy)
    local_e.start()

    @pl.when(native)
    def _():
        loop(0, 4, lambda i: local_t(i).start())

    barrier = pltpu.get_barrier_semaphore()
    for device in (left, right):
        pl.semaphore_signal(barrier, inc=1, device_id=device, device_id_type=MESH)

    def greet(i):
        device = (((xh + i // FEATS) % 2) * ZS + z, (fi + i) % FEATS)
        pl.semaphore_signal(barrier, inc=1, device_id=device, device_id_type=MESH)

    loop(1, 2 * FEATS, greet)
    pl.semaphore_wait(barrier, 2 * FEATS + 1)

    def swap_t(i):
        return remote(t_hbm.at[own_rows(i)], g.at[own_rows(i)], t_send.at[i], own_recv.at[i], partner)

    def swap_q(i):
        return remote(q_hbm.at[q_rows(i)], qb.at[1, q_rows(i)], away_send.at[i], away_recv.at[i], partner)

    def pass_q(i):
        return remote(qb.at[1, q_rows(i)], qb.at[1, q_rows(i)], fwd_send.at[i], away_recv.at[i], sibling)

    def share_q(i):
        return remote(q_hbm.at[q_rows(i)], qb.at[0, q_rows(i)], home_send.at[i], home_recv.at[i], sibling)

    def to_right(j, src):
        return remote(g.at[rows(src, CHUNK)], g.at[rows((j + 2) * PAIR, CHUNK)], r_send.at[j], r_recv.at[j], right)

    def to_left(j, src):
        return remote(g.at[rows(src, CHUNK)], g.at[rows((j + 2) * PAIR + CHUNK, CHUNK)], l_send.at[j], l_recv.at[j], left)

    def first_chunk(i):
        arrived(g.at[own_rows(i)], own_recv.at[i])
        to_right(i, i * CHUNK).start()
        to_left(i, i * CHUNK).start()

    @pl.when(foreign)
    def _():
        loop(0, 4, lambda i: swap_t(i).start())

    @pl.when(native)
    def _():
        loop(0, 4, first_chunk)

    share_e = remote(e_hbm, eb.at[c], e_send, e_recv, sibling)
    share_e.start()

    @pl.when(native)
    def _():
        def share(i):
            local_q(i).start()
            share_q(i).start()

        loop(0, QPARTS, share)

    layer = lax.broadcasted_iota(jnp.int32, (LAYERS, 128), 0)
    lane = lax.broadcasted_iota(jnp.int32, (LAYERS, 128), 1)
    low = jnp.zeros((LAYERS, 128), jnp.int32)
    high = jnp.zeros((LAYERS, 128), jnp.int32)
    for n in range(LAYERS):
        low = jnp.where(layer == n, offs[n], low)
        high = jnp.where(layer == n, offs[n + 1], high)

    def member(first):
        ids = lane + first
        return (ids >= low) & (ids < high)

    local_e.wait()

    def add_tile(i, acc):
        tile = eb[c, :, rows(i * 128, 128)]
        return acc + jnp.where(member(fi * WIDTH + i * 128), tile, 0.0)

    ls[fi] = lax.fori_loop(0, WIDTH // 128, add_tile, jnp.zeros((LAYERS, 128), jnp.float32))

    def share_sums(i):
        return remote(ls.at[fi], ls.at[fi], ls_send.at[i], ls_recv.at[fi], (qi, (fi + i) % FEATS))

    loop(1, FEATS, lambda i: share_sums(i).start())

    @pl.when(foreign)
    def _():
        first_chunk(0)
        first_chunk(1)
        swap_q(0).start()
        first_chunk(2)
        swap_q(1).start()
        first_chunk(3)
        swap_q(2).start()

    def take_sums(i):
        source = (fi + i) % FEATS
        arrived(ls.at[source], ls_recv.at[source])

    loop(1, FEATS, take_sums)
    layer_sum = jnp.sum(jnp.sum(ls[...], axis=0), axis=1, keepdims=True)
    total = jnp.sum(layer_sum, axis=0, keepdims=True)
    counts = (high - low).astype(jnp.float32)
    damping = 0.05 * (layer_sum / counts + total / F)

    arrived(eb.at[1 - c], e_recv)
    first_feature = (xl * 8 + y * 2 + xh) * WIDTH

    def weigh(i):
        at = rows(i * 128, 128)
        damp = jnp.sum(jnp.where(member(first_feature + i * 128), damping, 0.0), axis=0, keepdims=True)
        wt[:, at] = 1.0 / (eb[xh, :, at] + damp)

    loop(0, WIDTH // 128, weigh)

    def score_copies(p, side, half):
        distance = (p + 2) // 4
        source_z = (z + ZS + (2 * side - 1) * distance) % ZS
        part = jnp.where(p < 2, 2 * p + side, (p + 2) % 4 + 2 * side * (p // 14))
        device = (((xh + half) % 2) * ZS + z, c * 8 + source_z)
        src = pb.at[half, rows(p * PAIR + side * CHUNK, CHUNK)]
        dst = rb.at[slot, rows(part * CHUNK, CHUNK)]
        recv = o_recv.at[slot * 4 + part]
        send = o_send.at[half * (2 * PAIRS) + 2 * p + side]
        mine = jnp.logical_and(half == 0, fi == c * 8 + source_z)
        return mine, src, dst, send, recv, device

    def send_scores(p, side, half):
        mine, src, dst, send, recv, device = score_copies(p, side, half)

        @pl.when(mine)
        def _():
            pltpu.make_async_copy(src, dst, recv).start()

        @pl.when(jnp.logical_not(mine))
        def _():
            remote(src, dst, send, recv, device).start()

    def multiply(start, size, half):
        for n in range(QROWS // 256):
            scores = lax.dot_general(
                w[rows(start, size), :],
                qb[half, n * 256 : (n + 1) * 256, :],
                (((1,), (1,)), ((), ())),
                preferred_element_type=jnp.float32,
            )
            pb[half, rows(start, size), n * 256 : (n + 1) * 256] = scores.astype(jnp.bfloat16)

    def backlog(b):
        multiply(b * (GROUP * PAIR), GROUP * PAIR, 1)

        def send_both(i):
            send_scores(b * GROUP + i // 2, i % 2, 1)

        loop(0, 2 * GROUP, send_both)

    loop(0, QPARTS, lambda i: arrived(qb.at[0, q_rows(i)], home_recv.at[i]))

    def work(p):
        k = p - 2

        @pl.when(p >= 2)
        def _():
            arrived(g.at[rows(p * PAIR, CHUNK)], r_recv.at[k])
            arrived(g.at[rows(p * PAIR + CHUNK, CHUNK)], l_recv.at[k])

        @pl.when(jnp.logical_and(p >= 4, p < 14))
        def _():
            to_right(p, (p - 2) * PAIR).start()
            to_left(p, (p - 2 + 2 * (p // 12)) * PAIR + CHUNK).start()

        @pl.when(jnp.logical_and(foreign, jnp.logical_and(p >= 2, p < 7)))
        def _():
            swap_q(p - 2).wait_send()
            swap_q(p + 1).start()

        @pl.when(jnp.logical_and(foreign, jnp.logical_and(p >= 5, p < 13)))
        def _():
            arrived(qb.at[1, q_rows(p - 5)], away_recv.at[p - 5])
            pass_q(p - 5).start()

        def weight_rows(i):
            at = rows(i * 512, 512)
            raw = g[rows(p * PAIR, PAIR), at].astype(jnp.float32)
            w[rows(p * PAIR, PAIR), at] = (raw * wt[:, at]).astype(jnp.bfloat16)

        loop(0, WIDTH // 512, weight_rows)

        @pl.when(jnp.logical_and(native, p == BOTH))
        def _():
            loop(0, QPARTS, lambda i: arrived(qb.at[1, q_rows(i)], away_recv.at[i]))

        def one_half(half):
            multiply(p * PAIR, PAIR, half)
            send_scores(p, 0, half)
            send_scores(p, 1, half)

        loop(0, 1 + p // BOTH, one_half)

        @pl.when(p == BOTH)
        def _():
            loop(0, 2, backlog)

        @pl.when(p == BOTH + 1)
        def _():
            backlog(2)

    loop(0, PAIRS, work)

    def drain_scores(i):
        mine, src, dst, send, recv, device = score_copies((i % 32) // 2, i % 2, i // 32)

        @pl.when(jnp.logical_not(mine))
        def _():
            remote(src, dst, send, recv, device).wait_send()

    def drain_ring(j):
        to_right(j, 0).wait_send()
        to_left(j, 0).wait_send()

    loop(0, STEPS, drain_ring)
    loop(1, FEATS, lambda i: share_sums(i).wait_send())
    share_e.wait_send()

    @pl.when(native)
    def _():
        loop(0, QPARTS, lambda i: share_q(i).wait_send())

    @pl.when(foreign)
    def _():
        loop(0, 4, lambda i: swap_t(i).wait_send())
        loop(5, QPARTS, lambda i: swap_q(i).wait_send())
        loop(0, QPARTS, lambda i: pass_q(i).wait_send())

    loop(0, 4 * PAIRS, drain_scores)

    def finish(i):
        part = (i % 2) * 2 + i // 2
        at = rows(part * CHUNK, CHUNK)
        out[at, :] = jnp.zeros((CHUNK, QROWS), jnp.float32)

        def add(s):
            arrived(rb.at[s, at], o_recv.at[s * 4 + part])
            out[at, :] += rb[s, at, :].astype(jnp.float32)

        loop(0, CHIPS, add)

    loop(0, 4, finish)


def per_device(query_grads, train_grads, eigenvalues, offsets):
    dma = pltpu.SemaphoreType.DMA
    anywhere = pl.BlockSpec(memory_space=pl.ANY)
    return pl.pallas_call(
        kernel,
        out_shape=jax.ShapeDtypeStruct((ROWS, QROWS), jnp.float32),
        in_specs=[pl.BlockSpec(memory_space=pltpu.SMEM), anywhere, anywhere, anywhere],
        out_specs=pl.BlockSpec(memory_space=pltpu.VMEM),
        scratch_shapes=[
            pltpu.VMEM((PAIRS * PAIR, WIDTH), jnp.bfloat16),
            pltpu.VMEM((PAIRS * PAIR, WIDTH), jnp.bfloat16),
            pltpu.VMEM((2, QROWS, WIDTH), jnp.bfloat16),
            pltpu.VMEM((2, PAIRS * PAIR, QROWS), jnp.bfloat16),
            pltpu.VMEM((CHIPS, ROWS, QROWS), jnp.bfloat16),
            pltpu.VMEM((1, WIDTH), jnp.float32),
            pltpu.VMEM((2, 1, WIDTH), jnp.float32),
            pltpu.VMEM((FEATS, LAYERS, 128), jnp.float32),
            dma((4,)), dma((4,)),
            dma((STEPS,)), dma((STEPS,)), dma((STEPS,)), dma((STEPS,)),
            dma((QPARTS,)), dma((QPARTS,)), dma((QPARTS,)), dma((QPARTS,)), dma((QPARTS,)),
            dma, dma, dma,
            dma((FEATS,)), dma((FEATS,)),
            dma((4 * PAIRS,)), dma((4 * CHIPS,)),
        ],
        compiler_params=pltpu.CompilerParams(
            collective_id=0, has_side_effects=True, vmem_limit_bytes=56 * 2**20
        ),
        name="scores",
    )(offsets, query_grads, train_grads, eigenvalues.reshape(1, WIDTH))


def solution(mesh):
    return jax.shard_map(
        per_device,
        mesh=mesh,
        in_specs=(P("query", "feat"), P("query", "feat"), P("feat"), P()),
        out_specs=P("feat", "query"),
        check_vma=False,
    )
```

time: 349 us -> 117 us (0.34)
  the two profiles are of different devices: /device:TPU:17 before, /device:TPU:8 now
where the time goes in v1:
time: 117 us
  Pallas kernels  115 us (98%)
  local copies, waits for them, and re-layouts  1.67 us (1%)
    pallas_call x1, Pallas kernels, per_device(): pl.pallas_call(kernel, out_shape=jax.ShapeDtypeStruct((ROWS, QROWS), jnp....  115 us

profile of v1, /device:TPU:8, one launch (start us, length us, event | category | flops | bytes accessed | tf_op | source)
XLA Modules:
  0.0 117.1 jit_solution(13295754828851290271)
XLA Ops:
  0.0 115.5 %scores.1 = f32[128,512]{1,0:T(8,128)} custom-call(s32[33]{0:T(128)} %offs.1, bf16[512,4096]{1,0:T(8,128)(2,1)} %q_hbm.1, bf16[128,4096]{1,0:T(8,128)(2,1)} %t_hbm.1, f32[1,4096]{1,0:T(1,128)} %bitcast.1), custom_call_target="tpu_custom_call" | custom-call | tf_op jit(solution)/shard_map/scores/pallas_call | solution.py:331
  115.5 1.7 %copy.6 = f32[128,512]{1,0:T(8,128)} copy(f32[128,512]{1,0:T(8,128)} %scores.1) | data formatting | bytes 524288

commit v2 on v1

--- a/solution.py
+++ b/solution.py
@@ -106,23 +106,25 @@
         return remote(q_hbm.at[q_rows(i)], qb.at[0, q_rows(i)], home_send.at[i], home_recv.at[i], sibling)
 
     def to_right(j, src):
-        return remote(g.at[rows(src, CHUNK)], g.at[rows((j + 2) * PAIR, CHUNK)], r_send.at[j], r_recv.at[j], right)
+        return remote(g.at[rows(src, CHUNK)], g.at[rows((j + 2) * PAIR, CHUNK)], r_send, r_recv.at[j], right)
 
     def to_left(j, src):
-        return remote(g.at[rows(src, CHUNK)], g.at[rows((j + 2) * PAIR + CHUNK, CHUNK)], l_send.at[j], l_recv.at[j], left)
+        return remote(g.at[rows(src, CHUNK)], g.at[rows((j + 2) * PAIR + CHUNK, CHUNK)], l_send, l_recv.at[j], left)
 
     def first_chunk(i):
         arrived(g.at[own_rows(i)], own_recv.at[i])
         to_right(i, i * CHUNK).start()
-        to_left(i, i * CHUNK).start()
+        to_left((i + 2) % 4, i * CHUNK).start()
 
     @pl.when(foreign)
     def _():
-        loop(0, 4, lambda i: swap_t(i).start())
+        for i in (0, 2, 1, 3):
+            swap_t(i).start()
 
     @pl.when(native)
     def _():
-        loop(0, 4, first_chunk)
+        for i in (0, 2, 1, 3):
+            first_chunk(i)
 
     share_e = remote(e_hbm, eb.at[c], e_send, e_recv, sibling)
     share_e.start()
@@ -156,25 +158,21 @@
     ls[fi] = lax.fori_loop(0, WIDTH // 128, add_tile, jnp.zeros((LAYERS, 128), jnp.float32))
 
     def share_sums(i):
-        return remote(ls.at[fi], ls.at[fi], ls_send.at[i], ls_recv.at[fi], (qi, (fi + i) % FEATS))
+        return remote(ls.at[fi], ls.at[fi], ls_send, ls_recv, (qi, (fi + i) % FEATS))
 
     loop(1, FEATS, lambda i: share_sums(i).start())
 
     @pl.when(foreign)
     def _():
         first_chunk(0)
+        first_chunk(2)
+        swap_q(0).start()
         first_chunk(1)
-        swap_q(0).start()
-        first_chunk(2)
         swap_q(1).start()
         first_chunk(3)
         swap_q(2).start()
 
-    def take_sums(i):
-        source = (fi + i) % FEATS
-        arrived(ls.at[source], ls_recv.at[source])
-
-    loop(1, FEATS, take_sums)
+    arrived(ls.at[pl.ds(0, FEATS - 1)], ls_recv)
     layer_sum = jnp.sum(jnp.sum(ls[...], axis=0), axis=1, keepdims=True)
     total = jnp.sum(layer_sum, axis=0, keepdims=True)
     counts = (high - low).astype(jnp.float32)
@@ -191,14 +189,16 @@
     loop(0, WIDTH // 128, weigh)
 
     def score_copies(p, side, half):
-        distance = (p + 2) // 4
+        late = p // 12
+        distance = jnp.where(late > 0, 4 - p % 2, (p + 2) // 4)
+        number = jnp.where(late > 0, p % 2 * 2 + (p - 12) // 2, (p + 2) % 4)
         source_z = (z + ZS + (2 * side - 1) * distance) % ZS
-        part = jnp.where(p < 2, 2 * p + side, (p + 2) % 4 + 2 * side * (p // 14))
+        part = jnp.where(p < 2, 2 * p + side, (number + 2 * side) % 4)
         device = (((xh + half) % 2) * ZS + z, c * 8 + source_z)
         src = pb.at[half, rows(p * PAIR + side * CHUNK, CHUNK)]
         dst = rb.at[slot, rows(part * CHUNK, CHUNK)]
-        recv = o_recv.at[slot * 4 + part]
-        send = o_send.at[half * (2 * PAIRS) + 2 * p + side]
+        recv = o_recv.at[part]
+        send = o_send
         mine = jnp.logical_and(half == 0, fi == c * 8 + source_z)
         return mine, src, dst, send, recv, device
 
@@ -214,22 +214,23 @@
             remote(src, dst, send, recv, device).start()
 
     def multiply(start, size, half):
+        at = pl.ds(pl.multiple_of(start, PAIR), size)
         for n in range(QROWS // 256):
             scores = lax.dot_general(
-                w[rows(start, size), :],
+                w[at, :],
                 qb[half, n * 256 : (n + 1) * 256, :],
                 (((1,), (1,)), ((), ())),
                 preferred_element_type=jnp.float32,
             )
-            pb[half, rows(start, size), n * 256 : (n + 1) * 256] = scores.astype(jnp.bfloat16)
-
-    def backlog(b):
-        multiply(b * (GROUP * PAIR), GROUP * PAIR, 1)
+            pb[half, at, n * 256 : (n + 1) * 256] = scores.astype(jnp.bfloat16)
+
+    def backlog(b, size=GROUP):
+        multiply(b * (GROUP * PAIR), size * PAIR, 1)
 
         def send_both(i):
             send_scores(b * GROUP + i // 2, i % 2, 1)
 
-        loop(0, 2 * GROUP, send_both)
+        loop(0, 2 * size, send_both)
 
     loop(0, QPARTS, lambda i: arrived(qb.at[0, q_rows(i)], home_recv.at[i]))
 
@@ -241,10 +242,18 @@
             arrived(g.at[rows(p * PAIR, CHUNK)], r_recv.at[k])
             arrived(g.at[rows(p * PAIR + CHUNK, CHUNK)], l_recv.at[k])
 
-        @pl.when(jnp.logical_and(p >= 4, p < 14))
-        def _():
-            to_right(p, (p - 2) * PAIR).start()
-            to_left(p, (p - 2 + 2 * (p // 12)) * PAIR + CHUNK).start()
+        def pass_on(j, pair):
+            to_right(j, pair * PAIR).start()
+            to_left(j, pair * PAIR + CHUNK).start()
+
+        @pl.when(jnp.logical_and(p >= 2, p < 8))
+        def _():
+            pass_on(p + 2, p)
+
+        @pl.when(jnp.logical_or(p == 10, p == 11))
+        def _():
+            pass_on(2 * p - 10, p)
+            pass_on(2 * p - 9, p - 2)
 
         @pl.when(jnp.logical_and(foreign, jnp.logical_and(p >= 2, p < 7)))
         def _():
@@ -280,23 +289,29 @@
 
         @pl.when(p == BOTH + 1)
         def _():
-            backlog(2)
+            backlog(2, BOTH - 2 * GROUP)
 
     loop(0, PAIRS, work)
 
-    def drain_scores(i):
-        mine, src, dst, send, recv, device = score_copies((i % 32) // 2, i % 2, i // 32)
-
-        @pl.when(jnp.logical_not(mine))
-        def _():
-            remote(src, dst, send, recv, device).wait_send()
-
-    def drain_ring(j):
-        to_right(j, 0).wait_send()
-        to_left(j, 0).wait_send()
-
-    loop(0, STEPS, drain_ring)
-    loop(1, FEATS, lambda i: share_sums(i).wait_send())
+    for part in (0, 2, 1, 3):
+        at = pl.ds(part * CHUNK, CHUNK)
+        arrived(rb.at[:, at], o_recv.at[part])
+        total = rb[0, at, :].astype(jnp.float32)
+        for source in range(1, CHIPS):
+            total += rb[source, at, :].astype(jnp.float32)
+        out[at, :] = total
+
+    sent = pl.ds(0, STEPS * CHUNK)
+    arrived(g.at[sent], r_send)
+    arrived(g.at[sent], l_send)
+    arrived(pb.at[0], o_send)
+    arrived(pb.at[1, pl.ds(0, (PAIRS - 2) * PAIR)], o_send)
+
+    @pl.when(xl != c)
+    def _():
+        arrived(pb.at[1, pl.ds((PAIRS - 2) * PAIR, 2 * PAIR)], o_send)
+
+    arrived(ls.at[pl.ds(0, FEATS - 1)], ls_send)
     share_e.wait_send()
 
     @pl.when(native)
@@ -308,21 +323,6 @@
         loop(0, 4, lambda i: swap_t(i).wait_send())
         loop(5, QPARTS, lambda i: swap_q(i).wait_send())
         loop(0, QPARTS, lambda i: pass_q(i).wait_send())
-
-    loop(0, 4 * PAIRS, drain_scores)
-
-    def finish(i):
-        part = (i % 2) * 2 + i // 2
-        at = rows(part * CHUNK, CHUNK)
-        out[at, :] = jnp.zeros((CHUNK, QROWS), jnp.float32)
-
-        def add(s):
-            arrived(rb.at[s, at], o_recv.at[s * 4 + part])
-            out[at, :] += rb[s, at, :].astype(jnp.float32)
-
-        loop(0, CHIPS, add)
-
-    loop(0, 4, finish)
 
 
 def per_device(query_grads, train_grads, eigenvalues, offsets):
@@ -343,11 +343,11 @@
             pltpu.VMEM((2, 1, WIDTH), jnp.float32),
             pltpu.VMEM((FEATS, LAYERS, 128), jnp.float32),
             dma((4,)), dma((4,)),
-            dma((STEPS,)), dma((STEPS,)), dma((STEPS,)), dma((STEPS,)),
+            dma, dma((STEPS,)), dma, dma((STEPS,)),
             dma((QPARTS,)), dma((QPARTS,)), dma((QPARTS,)), dma((QPARTS,)), dma((QPARTS,)),
             dma, dma, dma,
-            dma((FEATS,)), dma((FEATS,)),
-            dma((4 * PAIRS,)), dma((4 * CHIPS,)),
+            dma, dma,
+            dma, dma((4,)),
         ],
         compiler_params=pltpu.CompilerParams(
             collective_id=0, has_side_effects=True, vmem_limit_bytes=56 * 2**20

time: 117 us -> 111 us (0.949)
  the two profiles are of different devices: /device:TPU:8 before, /device:TPU:17 now
where the time goes in v2:
time: 111 us; the launch traced here: 109 us
  Pallas kernels  108 us (97%)
  local copies, waits for them, and re-layouts  1.67 us (2%)
    pallas_call x1, Pallas kernels, per_device(): pl.pallas_call(kernel, out_shape=jax.ShapeDtypeStruct((ROWS, QROWS), jnp....  108 us

profile of v2, /device:TPU:17, one launch (start us, length us, event | category | flops | bytes accessed | tf_op | source)
XLA Modules:
  0.0 109.2 jit_solution(1038151466832440187)
XLA Ops:
  0.0 107.5 %scores.1 = f32[128,512]{1,0:T(8,128)} custom-call(s32[33]{0:T(128)} %offs.1, bf16[512,4096]{1,0:T(8,128)(2,1)} %q_hbm.1, bf16[128,4096]{1,0:T(8,128)(2,1)} %t_hbm.1, f32[1,4096]{1,0:T(1,128)} %bitcast.1), custom_call_target="tpu_custom_call" | custom-call | tf_op jit(solution)/shard_map/scores/pallas_call | solution.py:331
  107.5 1.7 %copy.6 = f32[128,512]{1,0:T(8,128)} copy(f32[128,512]{1,0:T(8,128)} %scores.1) | data formatting | bytes 524288

commit v3 on v2

--- a/solution.py
+++ b/solution.py
@@ -23,6 +23,7 @@
 QPARTS = 8
 QCHUNK = QROWS // QPARTS
 GROUP = 4
+SOME = 8
 BOTH = 12
 
 
@@ -188,49 +189,48 @@
 
     loop(0, WIDTH // 128, weigh)
 
-    def score_copies(p, side, half):
+    def send_scores(p, side, half, columns=pl.ds(0, QROWS)):
         late = p // 12
         distance = jnp.where(late > 0, 4 - p % 2, (p + 2) // 4)
         number = jnp.where(late > 0, p % 2 * 2 + (p - 12) // 2, (p + 2) % 4)
         source_z = (z + ZS + (2 * side - 1) * distance) % ZS
         part = jnp.where(p < 2, 2 * p + side, (number + 2 * side) % 4)
-        device = (((xh + half) % 2) * ZS + z, c * 8 + source_z)
-        src = pb.at[half, rows(p * PAIR + side * CHUNK, CHUNK)]
-        dst = rb.at[slot, rows(part * CHUNK, CHUNK)]
-        recv = o_recv.at[part]
-        send = o_send
         mine = jnp.logical_and(half == 0, fi == c * 8 + source_z)
-        return mine, src, dst, send, recv, device
-
-    def send_scores(p, side, half):
-        mine, src, dst, send, recv, device = score_copies(p, side, half)
+        src = pb.at[half, rows(p * PAIR + side * CHUNK, CHUNK), columns]
+        dst = rb.at[slot, rows(part * CHUNK, CHUNK), columns]
 
         @pl.when(mine)
         def _():
-            pltpu.make_async_copy(src, dst, recv).start()
+            pltpu.make_async_copy(src, dst, o_recv.at[part]).start()
 
         @pl.when(jnp.logical_not(mine))
         def _():
-            remote(src, dst, send, recv, device).start()
-
-    def multiply(start, size, half):
-        at = pl.ds(pl.multiple_of(start, PAIR), size)
-        for n in range(QROWS // 256):
-            scores = lax.dot_general(
-                w[at, :],
-                qb[half, n * 256 : (n + 1) * 256, :],
-                (((1,), (1,)), ((), ())),
-                preferred_element_type=jnp.float32,
-            )
-            pb[half, at, n * 256 : (n + 1) * 256] = scores.astype(jnp.bfloat16)
-
-    def backlog(b, size=GROUP):
-        multiply(b * (GROUP * PAIR), size * PAIR, 1)
-
-        def send_both(i):
-            send_scores(b * GROUP + i // 2, i % 2, 1)
-
-        loop(0, 2 * size, send_both)
+            device = (((xh + half) % 2) * ZS + z, c * 8 + source_z)
+            remote(src, dst, o_send, o_recv.at[part], device).start()
+
+    def multiply(start, size, block):
+        half, at, columns = block // 2, pl.ds(pl.multiple_of(start, PAIR), size), rows(block % 2 * 256, 256)
+        scores = lax.dot_general(
+            w[at, :], qb[half, columns, :], (((1,), (1,)), ((), ())), preferred_element_type=jnp.float32
+        )
+        pb[half, at, columns] = scores.astype(jnp.bfloat16)
+
+    near = 1 - z % 2
+
+    def order(n, turn):
+        ring = jnp.where(n < 8, n - 2, jnp.where(n < turn, n - 6, jnp.where(n < 22, n - turn + 6, n - 12)))
+        same = jnp.logical_or(n < 8, jnp.logical_and(n >= turn, n < 22))
+        return jnp.where(n < 4, n // 2, ring), jnp.where(n < 4, n % 2, jnp.where(same, near, 1 - near))
+
+    def backlog(groups, block):
+        loop(0, groups, lambda b: multiply(b * (GROUP * PAIR), GROUP * PAIR, block))
+        count = 2 * GROUP * groups
+
+        def send(i):
+            p, side = order((i + count // 4 * y) % count, 14 if groups == 2 else 16)
+            send_scores(p, side, 1, pl.ds(block % 2 * 256, 256))
+
+        loop(0, count, send)
 
     loop(0, QPARTS, lambda i: arrived(qb.at[0, q_rows(i)], home_recv.at[i]))
 
@@ -260,10 +260,10 @@
             swap_q(p - 2).wait_send()
             swap_q(p + 1).start()
 
-        @pl.when(jnp.logical_and(foreign, jnp.logical_and(p >= 5, p < 13)))
-        def _():
-            arrived(qb.at[1, q_rows(p - 5)], away_recv.at[p - 5])
-            pass_q(p - 5).start()
+        @pl.when(jnp.logical_and(foreign, jnp.logical_and(p >= 4, p < 12)))
+        def _():
+            arrived(qb.at[1, q_rows(p - 4)], away_recv.at[p - 4])
+            pass_q(p - 4).start()
 
         def weight_rows(i):
             at = rows(i * 512, 512)
@@ -272,24 +272,36 @@
 
         loop(0, WIDTH // 512, weight_rows)
 
+        @pl.when(jnp.logical_and(native, p == SOME))
+        def _():
+            loop(0, QPARTS // 2, lambda i: arrived(qb.at[1, q_rows(i)], away_recv.at[i]))
+
         @pl.when(jnp.logical_and(native, p == BOTH))
         def _():
-            loop(0, QPARTS, lambda i: arrived(qb.at[1, q_rows(i)], away_recv.at[i]))
-
-        def one_half(half):
-            multiply(p * PAIR, PAIR, half)
-            send_scores(p, 0, half)
-            send_scores(p, 1, half)
-
-        loop(0, 1 + p // BOTH, one_half)
+            loop(QPARTS // 2, QPARTS, lambda i: arrived(qb.at[1, q_rows(i)], away_recv.at[i]))
+
+        def one_block(block):
+            multiply(p * PAIR, PAIR, block)
+
+            @pl.when(block % 2 == 1)
+            def _():
+                send_scores(p, 0, block // 2)
+                send_scores(p, 1, block // 2)
+
+            @pl.when(jnp.logical_and(block == 2, p < BOTH))
+            def _():
+                send_scores(p, 0, 1, pl.ds(0, 256))
+                send_scores(p, 1, 1, pl.ds(0, 256))
+
+        loop(0, 2 + p // SOME + p // BOTH, one_block)
+
+        @pl.when(p == SOME)
+        def _():
+            backlog(SOME // GROUP, 2)
 
         @pl.when(p == BOTH)
         def _():
-            loop(0, 2, backlog)
-
-        @pl.when(p == BOTH + 1)
-        def _():
-            backlog(2, BOTH - 2 * GROUP)
+            backlog(BOTH // GROUP, 3)
 
     loop(0, PAIRS, work)
 

time: 111 us -> 108 us (0.973); the launches traced: 109 us -> 107 us
  Pallas kernels: 108 us -> 106 us
    pallas_call x1, Pallas kernels: 108 us -> 106 us  [per_device(): pl.pallas_call(kernel, out_shape=jax.ShapeDtypeStruct((ROWS, QROWS), jnp....]
where the time goes in v3:
time: 108 us; the launch traced here: 107 us
  Pallas kernels  106 us (98%)
  local copies, waits for them, and re-layouts  1.67 us (2%)
    pallas_call x1, Pallas kernels, per_device(): pl.pallas_call(kernel, out_shape=jax.ShapeDtypeStruct((ROWS, QROWS), jnp....  106 us

profile of v3, /device:TPU:17, one launch (start us, length us, event | category | flops | bytes accessed | tf_op | source)
XLA Modules:
  0.0 107.4 jit_solution(422144876169817253)
XLA Ops:
  0.0 105.7 %scores.1 = f32[128,512]{1,0:T(8,128)} custom-call(s32[33]{0:T(128)} %offs.1, bf16[512,4096]{1,0:T(8,128)(2,1)} %q_hbm.1, bf16[128,4096]{1,0:T(8,128)(2,1)} %t_hbm.1, f32[1,4096]{1,0:T(1,128)} %bitcast.1), custom_call_target="tpu_custom_call" | custom-call | tf_op jit(solution)/shard_map/scores/pallas_call | solution.py:343
  105.7 1.7 %copy.6 = f32[128,512]{1,0:T(8,128)} copy(f32[128,512]{1,0:T(8,128)} %scores.1) | data formatting | bytes 524288

commit v4 on v3

--- a/solution.py
+++ b/solution.py
@@ -172,6 +172,7 @@
         swap_q(1).start()
         first_chunk(3)
         swap_q(2).start()
+        swap_q(3).start()
 
     arrived(ls.at[pl.ds(0, FEATS - 1)], ls_recv)
     layer_sum = jnp.sum(jnp.sum(ls[...], axis=0), axis=1, keepdims=True)
@@ -255,15 +256,15 @@
             pass_on(2 * p - 10, p)
             pass_on(2 * p - 9, p - 2)
 
-        @pl.when(jnp.logical_and(foreign, jnp.logical_and(p >= 2, p < 7)))
+        @pl.when(jnp.logical_and(foreign, jnp.logical_and(p >= 2, p < 6)))
         def _():
             swap_q(p - 2).wait_send()
-            swap_q(p + 1).start()
-
-        @pl.when(jnp.logical_and(foreign, jnp.logical_and(p >= 4, p < 12)))
-        def _():
-            arrived(qb.at[1, q_rows(p - 4)], away_recv.at[p - 4])
-            pass_q(p - 4).start()
+            swap_q(p + 2).start()
+
+        @pl.when(jnp.logical_and(foreign, jnp.logical_and(p >= 5, p < 13)))
+        def _():
+            arrived(qb.at[1, q_rows(p - 5)], away_recv.at[p - 5])
+            pass_q(p - 5).start()
 
         def weight_rows(i):
             at = rows(i * 512, 512)
@@ -333,7 +334,7 @@
     @pl.when(foreign)
     def _():
         loop(0, 4, lambda i: swap_t(i).wait_send())
-        loop(5, QPARTS, lambda i: swap_q(i).wait_send())
+        loop(4, QPARTS, lambda i: swap_q(i).wait_send())
         loop(0, QPARTS, lambda i: pass_q(i).wait_send())
 
 

time: 108 us -> 106 us (0.981)
  Pallas kernels: 106 us -> 104 us
    pallas_call x1, Pallas kernels: 106 us -> 104 us  [per_device(): pl.pallas_call(kernel, out_shape=jax.ShapeDtypeStruct((ROWS, QROWS), jnp....]
where the time goes in v4:
time: 106 us
  Pallas kernels  104 us (98%)
  local copies, waits for them, and re-layouts  1.67 us (2%)
    pallas_call x1, Pallas kernels, per_device(): pl.pallas_call(kernel, out_shape=jax.ShapeDtypeStruct((ROWS, QROWS), jnp....  104 us

profile of v4, /device:TPU:17, one launch (start us, length us, event | category | flops | bytes accessed | tf_op | source)
XLA Modules:
  0.0 105.7 jit_solution(8629161463554101086)
XLA Ops:
  0.0 104.0 %scores.1 = f32[128,512]{1,0:T(8,128)} custom-call(s32[33]{0:T(128)} %offs.1, bf16[512,4096]{1,0:T(8,128)(2,1)} %q_hbm.1, bf16[128,4096]{1,0:T(8,128)(2,1)} %t_hbm.1, f32[1,4096]{1,0:T(1,128)} %bitcast.1), custom_call_target="tpu_custom_call" | custom-call | tf_op jit(solution)/shard_map/scores/pallas_call | solution.py:344
  104.1 1.7 %copy.6 = f32[128,512]{1,0:T(8,128)} copy(f32[128,512]{1,0:T(8,128)} %scores.1) | data formatting | bytes 524288

commit v5 on v4

--- a/solution.py
+++ b/solution.py
@@ -173,6 +173,7 @@
         first_chunk(3)
         swap_q(2).start()
         swap_q(3).start()
+        swap_q(4).start()
 
     arrived(ls.at[pl.ds(0, FEATS - 1)], ls_recv)
     layer_sum = jnp.sum(jnp.sum(ls[...], axis=0), axis=1, keepdims=True)
@@ -256,10 +257,10 @@
             pass_on(2 * p - 10, p)
             pass_on(2 * p - 9, p - 2)
 
-        @pl.when(jnp.logical_and(foreign, jnp.logical_and(p >= 2, p < 6)))
+        @pl.when(jnp.logical_and(foreign, jnp.logical_and(p >= 2, p < 5)))
         def _():
             swap_q(p - 2).wait_send()
-            swap_q(p + 2).start()
+            swap_q(p + 3).start()
 
         @pl.when(jnp.logical_and(foreign, jnp.logical_and(p >= 5, p < 13)))
         def _():
@@ -334,7 +335,7 @@
     @pl.when(foreign)
     def _():
         loop(0, 4, lambda i: swap_t(i).wait_send())
-        loop(4, QPARTS, lambda i: swap_q(i).wait_send())
+        loop(3, QPARTS, lambda i: swap_q(i).wait_send())
         loop(0, QPARTS, lambda i: pass_q(i).wait_send())
 
 

time: 106 us -> 106 us (level)
  no operation moved by 1% of the time
where the time goes in v5:
time: 106 us
  Pallas kernels  104 us (98%)
  local copies, waits for them, and re-layouts  1.67 us (2%)
    pallas_call x1, Pallas kernels, per_device(): pl.pallas_call(kernel, out_shape=jax.ShapeDtypeStruct((ROWS, QROWS), jnp....  104 us

profile of v5, /device:TPU:17, one launch (start us, length us, event | category | flops | bytes accessed | tf_op | source)
XLA Modules:
  0.0 105.7 jit_solution(12452821605606578888)
XLA Ops:
  0.0 104.0 %scores.1 = f32[128,512]{1,0:T(8,128)} custom-call(s32[33]{0:T(128)} %offs.1, bf16[512,4096]{1,0:T(8,128)(2,1)} %q_hbm.1, bf16[128,4096]{1,0:T(8,128)(2,1)} %t_hbm.1, f32[1,4096]{1,0:T(1,128)} %bitcast.1), custom_call_target="tpu_custom_call" | custom-call | tf_op jit(solution)/shard_map/scores/pallas_call | solution.py:345
  104.0 1.7 %copy.6 = f32[128,512]{1,0:T(8,128)} copy(f32[128,512]{1,0:T(8,128)} %scores.1) | data formatting | bytes 524288
